TPU v7x, 128 devices: a whole 4x4x4 slice. The times are simulated.
128 devices in a mesh: row: 8 (over y, x_hi), col: 16 (over z, x_lo, core).
Axes of the slice: x: 4 (x_hi: 2, x_lo: 2; x = x_hi * 2 + x_lo), y: 4, z: 4, core: 2. Of those that a mesh axis runs over, the one named last changes fastest.
Arguments:
- new_row: float32 [128, 192, 128], P('row', 'col'), may hold values from -4 to 4
- history: float32 [192, 192, 128, 128], P('row', 'col'), may hold values from -0.0390625 to 0.0390625
- hamiltonian: float32 [128, 128], replicated, may hold values from -0.5 to 0.5
Outputs:
- rows_out: float32 [3, 128, 192, 128], P(None, 'row', 'col')
All inputs are finite; a program needn't handle non-finite values.
Results may differ from a plain program's by a relative error of at most 0.00026.
Values sent between devices are 32-bit elements; how exact they have to be, the bound alone decides.
A program may use at most 128 MiB of HBM per device.

v0:
```python
import jax
import jax.numpy as jnp
from jax import lax
from jax.sharding import PartitionSpec as P

STEPS = 3
time_step = 0.2


def sigma_panel(sigma_all, tile_rows):
    row_start = lax.axis_index("row") * tile_rows
    gathered = lax.all_gather(sigma_all, "col", axis=1, tiled=True)
    return lax.dynamic_slice_in_dim(gathered, row_start, tile_rows, 1)


def contract(sigma_rows, history):
    return jnp.einsum(
        "isl,stlj->itj",
        sigma_rows,
        history,
        precision=lax.Precision.HIGHEST,
        preferred_element_type=jnp.float32,
    )


def advance(current, hamiltonian, collision):
    kinetic = jnp.einsum(
        "itl,lj->itj",
        current,
        hamiltonian,
        precision=lax.Precision.HIGHEST,
        preferred_element_type=jnp.float32,
    )
    return current - time_step * (kinetic + collision)


def per_device(new_row, history, hamiltonian):
    tile_rows = history.shape[0]
    results = []
    current = new_row
    for step_index in range(STEPS):
        sigma_local = current * current * current
        sigma_all = lax.all_gather(sigma_local, "row", axis=0, tiled=True)
        sigma_rows = sigma_panel(sigma_all, tile_rows)
        collision = lax.psum_scatter(
            contract(sigma_rows, history), "row", scatter_dimension=0, tiled=True
        )
        current = advance(current, hamiltonian, collision)
        results.append(current)
    return jnp.stack(results)


def solution(mesh):
    placed = (P("row", "col", None), P("row", "col", None, None), P())
    return jax.shard_map(
        per_device,
        mesh=mesh,
        in_specs=placed,
        out_specs=P(None, "row", "col", None),
        check_vma=False,
    )
```

profile of v0, /device:TPU:0, one launch (start us, length us, event | category | flops | bytes accessed | tf_op | source)
XLA Modules:
  0.0 612.5 jit_solution(13961219519606241692)
XLA Ops:
  6.5 0.0 copy-start
  6.5 0.0 copy-start.1
  6.5 0.0 all-gather.4.cloned.1.call-start
  6.5 1.0 multiply_multiply_fusion.2
  7.5 38.7 %all_gather.18 = f32[128,12,128]{2,0,1:T(8,128)} all-gather(f32[16,12,128]{2,0,1:T(8,128)S(1)} %multiply_multiply_fusion.2), channel_id=1, replica_groups=mesh['row'=8,'col'=16] {'row'}, dimensions={0}, use_global_device_ids=true | all-gather | bytes 884736 | tf_op jit(solution)/shard_map/all_gather | solution.py:43
  46.2 0.0 all-gather.4.cloned.1.call-update
  46.2 0.0 reduce-scatter.4.cloned.1.call-start
  46.3 74.7 %all-gather.4.cloned.1.call-done = f32[128,192,128]{2,0,1:T(8,128)} async-done(((f32[128,12,128]{2,0,1:T(8,128)}), f32[128,192,128]{2,0,1:T(8,128)}) %all-gather.4.cloned.1.call-update) | async-done | bytes 12582928 | tf_op jit(solution)/shard_map/all_gather | solution.py:12
  121.0 14.3 %fusion.9 = f32[128,12,128]{2,0,1:T(8,128)} fusion(f32[24,12,128,128]{3,2,1,0:T(8,128)} %param.4, f32[128,192,128]{2,0,1:T(8,128)} %all-gather.4.cloned.1.call-done, s32[]{:T(128)S(6)} %select_n.2), kind=kOutput, calls=%fused_computation.9 | convolution fusion | flops 7247757312 | bytes 21233668 | tf_op jit(solution)/shard_map/isl,stlj->itj/dot_general | solution.py:17
  135.3 0.0 reduce-scatter.4.cloned.1.call-update
  135.3 0.0 all-gather.6.cloned.1.call-start
  135.4 72.5 %reduce-scatter.4.cloned.1.call-done = f32[16,12,128]{2,0,1:T(8,128)} async-done(((f32[128,12,128]{2,0,1:T(8,128)}), f32[16,12,128]{2,0,1:T(8,128)}) %reduce-scatter.4.cloned.1.call-update) | async-done | bytes 98320 | tf_op jit(solution)/shard_map/reduce_scatter | solution.py:45
  207.8 0.0 copy-done
  207.9 0.0 copy-done.1
  207.9 1.1 multiply_multiply_fusion.1
  209.0 38.9 %all_gather.20 = f32[128,12,128]{2,0,1:T(8,128)} all-gather(f32[16,12,128]{2,0,1:T(8,128)S(1)} %get-tuple-element.5), channel_id=1, replica_groups=mesh['row'=8,'col'=16] {'row'}, dimensions={0}, use_global_device_ids=true | all-gather | bytes 884736 | tf_op jit(solution)/shard_map/all_gather | solution.py:43
  247.9 0.0 all-gather.6.cloned.1.call-update
  247.9 0.0 reduce-scatter.6.cloned.1.call-start
  248.0 71.0 %all-gather.6.cloned.1.call-done = f32[128,192,128]{2,0,1:T(8,128)} async-done(((f32[128,12,128]{2,0,1:T(8,128)}), f32[128,192,128]{2,0,1:T(8,128)}) %all-gather.6.cloned.1.call-update) | async-done | bytes 12582928 | tf_op jit(solution)/shard_map/all_gather | solution.py:12
  319.0 14.3 %fusion.12 = f32[128,12,128]{2,0,1:T(8,128)} fusion(f32[24,12,128,128]{3,2,1,0:T(8,128)} %param.4, f32[128,192,128]{2,0,1:T(8,128)} %all-gather.6.cloned.1.call-done, s32[]{:T(128)S(6)} %select_n.2), kind=kOutput, calls=%fused_computation.10 | convolution fusion | flops 7247757312 | bytes 21233668 | tf_op jit(solution)/shard_map/isl,stlj->itj/dot_general | solution.py:17
  333.3 0.0 reduce-scatter.6.cloned.1.call-update
  333.3 0.0 all-gather.8.cloned.1.call-start
  333.4 72.5 %reduce-scatter.6.cloned.1.call-done = f32[16,12,128]{2,0,1:T(8,128)} async-done(((f32[128,12,128]{2,0,1:T(8,128)}), f32[16,12,128]{2,0,1:T(8,128)}) %reduce-scatter.6.cloned.1.call-update) | async-done | bytes 98320 | tf_op jit(solution)/shard_map/reduce_scatter | solution.py:45
  405.9 1.1 multiply_multiply_fusion
  407.0 38.9 %all_gather.22 = f32[128,12,128]{2,0,1:T(8,128)} all-gather(f32[16,12,128]{2,0,1:T(8,128)S(1)} %get-tuple-element.7), channel_id=1, replica_groups=mesh['row'=8,'col'=16] {'row'}, dimensions={0}, use_global_device_ids=true | all-gather | bytes 884736 | tf_op jit(solution)/shard_map/all_gather | solution.py:43
  445.9 0.0 all-gather.8.cloned.1.call-update
  445.9 0.2 reduce-scatter.8.cloned.1.call-start
  446.2 70.8 %all-gather.8.cloned.1.call-done = f32[128,192,128]{2,0,1:T(8,128)} async-done(((f32[128,12,128]{2,0,1:T(8,128)}), f32[128,192,128]{2,0,1:T(8,128)}) %all-gather.8.cloned.1.call-update) | async-done | bytes 12582928 | tf_op jit(solution)/shard_map/all_gather | solution.py:12
  516.9 14.3 %fusion.15 = f32[128,12,128]{2,0,1:T(8,128)} fusion(f32[24,12,128,128]{3,2,1,0:T(8,128)} %param.4, f32[128,192,128]{2,0,1:T(8,128)} %all-gather.8.cloned.1.call-done, s32[]{:T(128)S(6)} %select_n.2), kind=kOutput, calls=%fused_computation.11 | convolution fusion | flops 7247757312 | bytes 21233668 | tf_op jit(solution)/shard_map/isl,stlj->itj/dot_general | solution.py:17
  531.3 0.0 reduce-scatter.8.cloned.1.call-update
  531.3 72.5 %reduce-scatter.8.cloned.1.call-done = f32[16,12,128]{2,0,1:T(8,128)} async-done(((f32[128,12,128]{2,0,1:T(8,128)}), f32[16,12,128]{2,0,1:T(8,128)}) %reduce-scatter.8.cloned.1.call-update) | async-done | bytes 98320 | tf_op jit(solution)/shard_map/reduce_scatter | solution.py:45
  603.8 1.1 fusion.20
  604.9 0.7 pad_maximum_fusion
Async XLA Ops:
  6.5 201.3 %copy-start = (f32[128,128]{1,0:T(8,128)S(1)}, f32[128,128]{1,0:T(8,128)}, u32[]{:S(2)}) copy-start(f32[128,128]{1,0:T(8,128)} %param.5) | copy-start | bytes 196612
  6.5 201.3 %copy-start.1 = (f32[16,12,128]{2,0,1:T(8,128)S(1)}, f32[16,12,128]{2,0,1:T(8,128)}, u32[]{:S(2)}) copy-start(f32[16,12,128]{2,0,1:T(8,128)} %param.3) | copy-start | bytes 294916
  6.5 114.4 %all-gather.4.cloned.1.call-start = ((), (), s32[]{:S(2)}) async-start(), calls=%async_computation.3 | async-start | bytes 13369344 | tf_op jit(solution)/shard_map/all_gather | solution.py:12
  46.2 161.7 %reduce-scatter.4.cloned.1.call-start = ((), (), s32[]{:S(2)}) async-start(), calls=%async_computation.4 | async-start | bytes 884736 | tf_op jit(solution)/shard_map/reduce_scatter | solution.py:45
  135.3 183.6 %all-gather.6.cloned.1.call-start = ((), (), s32[]{:S(2)}) async-start(), calls=%async_computation.5 | async-start | bytes 13369344 | tf_op jit(solution)/shard_map/all_gather | solution.py:12
  247.9 157.9 %reduce-scatter.6.cloned.1.call-start = ((), (), s32[]{:S(2)}) async-start(), calls=%async_computation.6 | async-start | bytes 884736 | tf_op jit(solution)/shard_map/reduce_scatter | solution.py:45
  333.3 183.6 %all-gather.8.cloned.1.call-start = ((), (), s32[]{:S(2)}) async-start(), calls=%async_computation.7 | async-start | bytes 13369344 | tf_op jit(solution)/shard_map/all_gather | solution.py:12
  445.9 157.9 %reduce-scatter.8.cloned.1.call-start = ((), (), s32[]{:S(2)}) async-start(), calls=%async_computation.8 | async-start | bytes 884736 | tf_op jit(solution)/shard_map/reduce_scatter | solution.py:45
Sparse Core Ops, SparseCore 0:
  46.3 74.6 all-gather.3
  135.4 72.3 reduce-scatter.3
  248.1 70.8 all-gather.5
  333.4 72.3 reduce-scatter.5
  446.1 70.8 all-gather.7
  531.4 72.3 reduce-scatter.7
where the time goes:
time: 613 us
  waiting for transfers between devices  434 us (71%)
  blocking collectives  116 us (19%)
  matrix products  46.4 us (8%)
  between operations  13.5 us (2%)
    reduce_scatter x3, waiting for transfers between devices, per_device(): lax.psum_scatter(contract(sigma_rows, history), 'row', scatter_dimension=...  217 us
    all_gather x3, waiting for transfers between devices, sigma_panel(): gathered = lax.all_gather(sigma_all, 'col', axis=1, tiled=True)  216 us
    all_gather x3, blocking collectives, per_device(): sigma_all = lax.all_gather(sigma_local, 'row', axis=0, tiled=True)  116 us
    dot_general x3, matrix products, contract(): jnp.einsum('isl,stlj->itj', sigma_rows, history, precision=lax.Precision....  43 us
  transfers between devices with their start and end apart: 6, of which 6 were waited for; matrix products, arithmetic and copies ran while one was open for 0% of the time, Pallas kernels for 0%

commit v1 on v0

--- a/solution.py
+++ b/solution.py
@@ -5,11 +5,20 @@
 
 STEPS = 3
 time_step = 0.2
+state_touch = lambda u_in, axis_key: jnp.concatenate(
+    lax.all_to_all(
+        jnp.stack([u_in for _ in range(lax.psum(1, axis_key))], axis=0),
+        axis_key,
+        split_axis=0,
+        concat_axis=0,
+    ),
+    axis=1,
+)
 
 
 def sigma_panel(sigma_all, tile_rows):
     row_start = lax.axis_index("row") * tile_rows
-    gathered = lax.all_gather(sigma_all, "col", axis=1, tiled=True)
+    gathered = state_touch(sigma_all, "col")
     return lax.dynamic_slice_in_dim(gathered, row_start, tile_rows, 1)
 
 

time: 613 us -> 825 us (1.35)
  blocking collectives: 116 us -> 401 us
  waiting for transfers between devices: 434 us -> 349 us
  local copies, waits for them, and re-layouts: 0.01 us -> 9.33 us
    all_to_all x0 -> x2, blocking collectives: none -> 290 us  [lax.all_to_all(jnp.stack([u_in for _ in range(lax.psum(1, axis_key))], ax...]
    all_gather x3 -> x0, waiting for transfers between devices: 216 us -> none  [sigma_panel(): gathered = lax.all_gather(sigma_all, 'col', axis=1, tiled=True)]
    all_to_all x0 -> x1, waiting for transfers between devices: none -> 140 us  [lax.all_to_all(jnp.stack([u_in for _ in range(lax.psum(1, axis_key))], ax...]
    another operation x0 -> x3, local copies, waits for them, and re-layouts: none -> 9.27 us  [jnp.stack([u_in for _ in range(lax.psum(1, axis_key))], axis=0)]
    reduce_scatter x3, waiting for transfers between devices: 217 us -> 209 us  [per_device(): lax.psum_scatter(contract(sigma_rows, history), 'row', scatter_dimension=...]
  transfers between devices with their start and end apart: 6 -> 4, of which waited for: 6 -> 4; matrix products, arithmetic and copies ran while one was open for 0% -> 0% of each run, Pallas kernels for 0% -> 0%
where the time goes in v1:
time: 825 us; the launch traced here: 824 us
  blocking collectives  401 us (49%)
  waiting for transfers between devices  349 us (42%)
  matrix products  42.7 us (5%)
  between operations  13.3 us (2%)
  local copies, waits for them, and re-layouts  9.33 us (1%)
    all_to_all x2, blocking collectives, lax.all_to_all(jnp.stack([u_in for _ in range(lax.psum(1, axis_key))], ax...  290 us
    reduce_scatter x3, waiting for transfers between devices, per_device(): lax.psum_scatter(contract(sigma_rows, history), 'row', scatter_dimension=...  209 us
    all_to_all x1, waiting for transfers between devices, lax.all_to_all(jnp.stack([u_in for _ in range(lax.psum(1, axis_key))], ax...  140 us
    all_gather x3, blocking collectives, per_device(): sigma_all = lax.all_gather(sigma_local, 'row', axis=0, tiled=True)  111 us
    dot_general x3, matrix products, contract(): jnp.einsum('isl,stlj->itj', sigma_rows, history, precision=lax.Precision....  39.3 us
  transfers between devices with their start and end apart: 4, of which 4 were waited for; matrix products, arithmetic and copies ran while one was open for 0% of the time, Pallas kernels for 0%

profile of v1, /device:TPU:0, one launch (start us, length us, event | category | flops | bytes accessed | tf_op | source)
XLA Modules:
  0.0 824.1 jit_solution(10472859751470623291)
XLA Ops:
  6.5 0.0 copy-start
  6.5 0.9 multiply_multiply_fusion.2
  7.5 37.0 %all_gather.9 = f32[128,12,128]{2,0,1:T(8,128)S(1)} all-gather(f32[16,12,128]{2,0,1:T(8,128)S(1)} %multiply_multiply_fusion.2), channel_id=1, replica_groups=mesh['row'=8,'col'=16] {'row'}, dimensions={0}, use_global_device_ids=true | all-gather | bytes 884736 | tf_op jit(solution)/shard_map/all_gather | solution.py:52
  44.5 6.1 stack.14
  50.6 6.9 all-to-all-start
  57.5 0.0 copy-start.1
  57.5 0.0 reduce-scatter.4.cloned.1.call-start
  57.6 140.2 %all-to-all-done = f32[16,128,12,128]{3,1,2,0:T(8,128)} async-done(((f32[16,128,12,128]{3,1,2,0:T(8,128)}), f32[16,128,12,128]{3,1,2,0:T(8,128)}, u32[]{:S(2)}, u32[]{:S(2)}) %all-to-all-start) | async-done | bytes 12582944 | tf_op jit(solution)/shard_map/all_to_all | solution.py:9
  197.8 14.3 %fusion.9 = f32[128,12,128]{2,0,1:T(8,128)} fusion(f32[24,12,128,128]{3,2,1,0:T(8,128)} %param.4, f32[128,192,128]{2,0,1:T(8,128)} %bitcast.2, s32[]{:T(128)S(6)} %select_n.2), kind=kOutput, calls=%fused_computation.9 | convolution fusion | flops 7247757312 | bytes 21233668 | tf_op jit(solution)/shard_map/isl,stlj->itj/dot_general | solution.py:26
  212.1 0.0 reduce-scatter.4.cloned.1.call-update
  212.1 0.0 reduce-scatter.6.cloned.1.call-start
  212.2 70.5 %reduce-scatter.4.cloned.1.call-done = f32[16,12,128]{2,0,1:T(8,128)} async-done(((f32[128,12,128]{2,0,1:T(8,128)}), f32[16,12,128]{2,0,1:T(8,128)}) %reduce-scatter.4.cloned.1.call-update) | async-done | bytes 98320 | tf_op jit(solution)/shard_map/reduce_scatter | solution.py:54
  282.7 0.0 copy-done
  282.7 0.0 copy-done.1
  282.7 1.1 multiply_multiply_fusion.1
  283.9 37.2 %all_gather.10 = f32[128,12,128]{2,0,1:T(8,128)S(1)} all-gather(f32[16,12,128]{2,0,1:T(8,128)S(1)} %get-tuple-element.5), channel_id=1, replica_groups=mesh['row'=8,'col'=16] {'row'}, dimensions={0}, use_global_device_ids=true | all-gather | bytes 884736 | tf_op jit(solution)/shard_map/all_gather | solution.py:52
  321.1 0.0 slice-start
  321.1 1.6 stack.16
  322.7 0.0 slice-start.2
  322.7 0.0 slice-start.3
  322.7 0.0 slice-start.4
  322.7 144.8 %all_to_all.15 = f32[16,128,12,128]{3,1,2,0:T(8,128)} all-to-all(f32[16,128,12,128]{3,1,2,0:T(8,128)S(1)} %stack.16), channel_id=1, replica_groups=mesh['row'=8,'col'=16] {'col'}, dimensions={0} | all-to-all | bytes 25165824 | tf_op jit(solution)/shard_map/all_to_all | solution.py:9
  467.5 0.0 slice-done
  467.5 0.0 slice-done.1
  467.5 0.0 slice-done.2
  467.5 0.0 slice-done.3
  467.5 0.0 slice-done.4
  467.6 12.5 %fusion.12 = f32[128,12,128]{2,0,1:T(8,128)} fusion(f32[24,12,128,128]{3,2,1,0:T(8,128)S(1)} %bitcast.67, f32[128,192,128]{2,0,1:T(8,128)} %bitcast.71, s32[]{:T(128)S(6)} %select_n.2), kind=kOutput, calls=%fused_computation.10 | convolution fusion | flops 7247757312 | bytes 21233668 | tf_op jit(solution)/shard_map/isl,stlj->itj/dot_general | solution.py:26
  480.1 0.0 reduce-scatter.6.cloned.1.call-update
  480.1 0.0 reduce-scatter.8.cloned.1.call-start
  480.1 69.1 %reduce-scatter.6.cloned.1.call-done = f32[16,12,128]{2,0,1:T(8,128)} async-done(((f32[128,12,128]{2,0,1:T(8,128)}), f32[16,12,128]{2,0,1:T(8,128)}) %reduce-scatter.6.cloned.1.call-update) | async-done | bytes 98320 | tf_op jit(solution)/shard_map/reduce_scatter | solution.py:54
  549.2 1.1 multiply_multiply_fusion
  550.4 37.3 %all_gather.11 = f32[128,12,128]{2,0,1:T(8,128)S(1)} all-gather(f32[16,12,128]{2,0,1:T(8,128)S(1)} %get-tuple-element.7), channel_id=1, replica_groups=mesh['row'=8,'col'=16] {'row'}, dimensions={0}, use_global_device_ids=true | all-gather | bytes 884736 | tf_op jit(solution)/shard_map/all_gather | solution.py:52
  587.6 1.6 stack.18
  589.2 0.0 slice-start.7
  589.2 0.0 slice-start.8
  589.2 0.0 slice-start.9
  589.2 144.8 %all_to_all.16 = f32[16,128,12,128]{3,1,2,0:T(8,128)} all-to-all(f32[16,128,12,128]{3,1,2,0:T(8,128)S(1)} %stack.18), channel_id=1, replica_groups=mesh['row'=8,'col'=16] {'col'}, dimensions={0} | all-to-all | bytes 25165824 | tf_op jit(solution)/shard_map/all_to_all | solution.py:9
  734.0 0.0 slice-done.5
  734.0 0.0 slice-done.6
  734.0 0.0 slice-done.7
  734.0 0.0 slice-done.8
  734.0 0.0 slice-done.9
  734.0 12.5 %fusion.15 = f32[128,12,128]{2,0,1:T(8,128)} fusion(f32[24,12,128,128]{3,2,1,0:T(8,128)S(1)} %bitcast.69, f32[128,192,128]{2,0,1:T(8,128)} %bitcast.70, s32[]{:T(128)S(6)} %select_n.2), kind=kOutput, calls=%fused_computation.11 | convolution fusion | flops 7247757312 | bytes 21233668 | tf_op jit(solution)/shard_map/isl,stlj->itj/dot_general | solution.py:26
  746.5 0.0 reduce-scatter.8.cloned.1.call-update
  746.6 69.2 %reduce-scatter.8.cloned.1.call-done = f32[16,12,128]{2,0,1:T(8,128)} async-done(((f32[128,12,128]{2,0,1:T(8,128)}), f32[16,12,128]{2,0,1:T(8,128)}) %reduce-scatter.8.cloned.1.call-update) | async-done | bytes 98320 | tf_op jit(solution)/shard_map/reduce_scatter | solution.py:54
  815.7 1.1 fusion.20
  816.9 0.7 pad_maximum_fusion
  (5 shorter events, 0.0 us)
Async XLA Ops:
  6.5 276.2 %copy-start = (f32[128,128]{1,0:T(8,128)S(1)}, f32[128,128]{1,0:T(8,128)}, u32[]{:S(2)}) copy-start(f32[128,128]{1,0:T(8,128)} %param.5) | copy-start | bytes 196612
  50.6 147.2 %all-to-all-start = ((f32[16,128,12,128]{3,1,2,0:T(8,128)}), f32[16,128,12,128]{3,1,2,0:T(8,128)}, u32[]{:S(2)}, u32[]{:S(2)}) async-start(f32[16,128,12,128]{3,1,2,0:T(8,128)} %stack.14), calls=%async_computation | async-start | bytes 25165824 | tf_op jit(solution)/shard_map/all_to_all | solution.py:9
  57.5 225.2 %copy-start.1 = (f32[16,12,128]{2,0,1:T(8,128)S(1)}, f32[16,12,128]{2,0,1:T(8,128)}, u32[]{:S(2)}) copy-start(f32[16,12,128]{2,0,1:T(8,128)} %param.3) | copy-start | bytes 294916
  57.5 225.2 %reduce-scatter.4.cloned.1.call-start = ((), (), s32[]{:S(2)}) async-start(), calls=%async_computation.6 | async-start | bytes 884736 | tf_op jit(solution)/shard_map/reduce_scatter | solution.py:54
  212.1 337.1 %reduce-scatter.6.cloned.1.call-start = ((), (), s32[]{:S(2)}) async-start(), calls=%async_computation.7 | async-start | bytes 884736 | tf_op jit(solution)/shard_map/reduce_scatter | solution.py:54
  321.1 146.4 %slice-start = ((s8[18874368]{0:T(1024)(128)(4,1)}), s8[4194304]{0:T(1024)(128)(4,1)S(1)}, s32[]{:S(2)}) async-start(s8[18874368]{0:T(1024)(128)(4,1)} %bitcast.66), calls=%async_computation.9 | async-start | bytes 8388608
  321.1 146.4 %slice-start.1 = ((s8[18874368]{0:T(1024)(128)(4,1)}), s8[2097152]{0:T(1024)(128)(4,1)S(1)}, s32[]{:S(2)}) async-start(s8[18874368]{0:T(1024)(128)(4,1)} %bitcast.66), calls=%async_computation.10 | async-start | bytes 4194304
  322.7 144.8 %slice-start.2 = ((s8[18874368]{0:T(1024)(128)(4,1)}), s8[4194304]{0:T(1024)(128)(4,1)S(1)}, s32[]{:S(2)}) async-start(s8[18874368]{0:T(1024)(128)(4,1)} %bitcast.66), calls=%async_computation.11 | async-start | bytes 8388608
  322.7 144.8 %slice-start.3 = ((s8[18874368]{0:T(1024)(128)(4,1)}), s8[4194304]{0:T(1024)(128)(4,1)S(1)}, s32[]{:S(2)}) async-start(s8[18874368]{0:T(1024)(128)(4,1)} %bitcast.66), calls=%async_computation.12 | async-start | bytes 8388608
  322.7 144.8 %slice-start.4 = ((s8[18874368]{0:T(1024)(128)(4,1)}), s8[4194304]{0:T(1024)(128)(4,1)S(1)}, s32[]{:S(2)}) async-start(s8[18874368]{0:T(1024)(128)(4,1)} %bitcast.66), calls=%async_computation.13 | async-start | bytes 8388608
  480.1 335.7 %reduce-scatter.8.cloned.1.call-start = ((), (), s32[]{:S(2)}) async-start(), calls=%async_computation.8 | async-start | bytes 884736 | tf_op jit(solution)/shard_map/reduce_scatter | solution.py:54
  587.6 146.4 %slice-start.5 = ((s8[18874368]{0:T(1024)(128)(4,1)}), s8[4194304]{0:T(1024)(128)(4,1)S(1)}, s32[]{:S(2)}) async-start(s8[18874368]{0:T(1024)(128)(4,1)} %bitcast.68), calls=%async_computation.14 | async-start | bytes 8388608
  587.6 146.4 %slice-start.6 = ((s8[18874368]{0:T(1024)(128)(4,1)}), s8[2097152]{0:T(1024)(128)(4,1)S(1)}, s32[]{:S(2)}) async-start(s8[18874368]{0:T(1024)(128)(4,1)} %bitcast.68), calls=%async_computation.15 | async-start | bytes 4194304
  589.2 144.8 %slice-start.7 = ((s8[18874368]{0:T(1024)(128)(4,1)}), s8[4194304]{0:T(1024)(128)(4,1)S(1)}, s32[]{:S(2)}) async-start(s8[18874368]{0:T(1024)(128)(4,1)} %bitcast.68), calls=%async_computation.16 | async-start | bytes 8388608
  589.2 144.8 %slice-start.8 = ((s8[18874368]{0:T(1024)(128)(4,1)}), s8[4194304]{0:T(1024)(128)(4,1)S(1)}, s32[]{:S(2)}) async-start(s8[18874368]{0:T(1024)(128)(4,1)} %bitcast.68), calls=%async_computation.17 | async-start | bytes 8388608
  589.2 144.8 %slice-start.9 = ((s8[18874368]{0:T(1024)(128)(4,1)}), s8[4194304]{0:T(1024)(128)(4,1)S(1)}, s32[]{:S(2)}) async-start(s8[18874368]{0:T(1024)(128)(4,1)} %bitcast.68), calls=%async_computation.18 | async-start | bytes 8388608
Sparse Core Ops, SparseCore 0:
  212.3 70.3 reduce-scatter.3
  480.2 68.9 reduce-scatter.5
  746.7 68.9 reduce-scatter.7
